TPU v7x, 32 devices: a whole 2x2x4 slice. The times are simulated.
32 devices in a mesh: blk: 8 (over y, x, core), grp: 4 (over z).
Axes of the slice: x: 2, y: 2, z: 4, core: 2. Of those that a mesh axis runs over, the one named last changes fastest.
Arguments:
- a_tiles: bfloat16 [256, 64, 1024], P(('blk', 'grp')), may hold values from -0.75 to 0.75
- a_cols: int32 [256, 16], P(('blk', 'grp')), may hold values from 0 to 255, as said below
- p_tiles: bfloat16 [256, 64, 256], P(('blk', 'grp')), may hold values from -0.75 to 0.75
- route_list: int32 [256, 256], P(('blk', 'grp')), may hold values from 0 to 255, as said below
- out_slot: int32 [32, 256], P(('blk', 'grp')), may hold values from 0 to 127, as said below
Outputs:
- coarse_blocks: float32 [4096, 4096], P(('blk', 'grp'))
Inputs may be any that keep to these rules, and one draw needn't show every extreme that they name: `a_cols`: fine block row f is held by device f // 8 of blk+grp. Every entry in the rows of one device names a fine block row held by a device with the same grp index, and among the 128 entries of one device's rows exactly 16 name rows held by each blk index. `route_list`: A value o * 64 + p sends the partial block to send position p for the device with grp index o and the same blk index. For each device and each o, no position at or above a count is used, the count being at least 16, and 64 for one o of each device. `out_slot`: entry o * 64 + p of row d is the output block, among the 128 of the device with grp index o and the blk index of device d, into which send position p of device d adds; each output block index stands exactly 4 * 64 // 128 times in a row.
All inputs are finite; a program needn't handle non-finite values.
Results may differ from a plain program's by a relative error of at most 0.0029.
Values may be sent and summed in bfloat16 or wider, within the bound.
No kernel may reach another device: no remote copies, remote signals or barrier semaphores. Data moves between devices by JAX's collectives and lax.ppermute only.
A program may use at most 128 MiB of HBM per device.

v0:
```python
import functools

import jax
import jax.numpy as jnp
from jax import lax
from jax.experimental import pallas as pl
from jax.experimental.pallas import tpu as pltpu
from jax.sharding import PartitionSpec as P

OSLOT = 128
LANES = 128
ACCS = 4
AHEAD = 2
NAME_ROWS = 16


def log2(n):
    assert n & (n - 1) == 0
    return n.bit_length() - 1


def partial_kernel(n_rows, n_pieces, spans, cap, groups, table_of, ints, *refs):
    row_parts, refs = refs[:n_rows], refs[n_rows:]
    pieces, refs = refs[:n_pieces], refs[n_pieces:]
    outs, refs = refs[:len(spans)], refs[len(spans):]
    accs, (a_ref, lhs_ref, panel, y_buf, w_buf, *rest, sems) = refs[:ACCS], refs[ACCS:]
    ints_ref, place_vmem, idx_vmem, place_ref, idx_ref = rest
    rf, tile, cols = a_ref.shape
    tiles = cols // tile
    width = panel.shape[2] // tile
    sub = tile * tile // LANES
    n_tables = accs[0].shape[0] // cap
    chunk = 8

    copies = [pltpu.make_async_copy(ints, ints_ref, sems.at[0])]
    for parts, whole in ((row_parts, a_ref), (pieces, panel)):
        at = 0
        for part in parts:
            height = part.shape[0]
            copies.append(
                pltpu.make_async_copy(part, whole.at[pl.ds(at, height)], sems.at[len(copies)])
            )
            at += height
    for copy in copies:
        copy.start()
    copies.pop(0).wait()

    me, blk = lax.axis_index("grp"), lax.axis_index("blk")
    n_places = width * tiles * width
    route, names = ints_ref[:rf, :n_places], ints_ref[rf:, :n_places].astype(jnp.float32)
    owner = lax.shift_right_logical(route, jnp.int32(log2(cap)))
    table = table_of(owner ^ me, (me == 1) | (me == 2))
    place_vmem[...] = jnp.where(table < n_tables, table * cap + (route & (cap - 1)), n_tables * cap)
    cols = ints_ref[:rf, n_places:]
    d = lax.shift_right_logical(cols, jnp.int32(log2(rf * groups))) ^ blk
    half = panel.shape[0] // (2 * rf)
    idx_vmem[:, :tiles] = ((d & 1) * half + lax.shift_right_logical(d, jnp.int32(1))) * rf + (cols & (rf - 1))
    for n, (src, dst) in enumerate(((place_vmem, place_ref), (idx_vmem, idx_ref))):
        copy = pltpu.make_async_copy(src, dst, sems.at[1 + n_rows + n_pieces + n])
        copy.start()
        copies.append(copy)

    def clear(c, carry):
        blocks = pl.ds(c * chunk, chunk)
        for acc in accs:
            acc[blocks] = jnp.zeros((chunk, sub, LANES), jnp.float32)
        return carry

    lax.fori_loop(0, n_tables * cap // chunk, clear, 0)
    for acc in accs:
        acc[n_tables * cap] = jnp.zeros((sub, LANES), jnp.float32)
    for copy in copies:
        copy.wait()

    columns = width * tile
    from_col = lax.broadcasted_iota(jnp.int32, (columns, columns), 0)
    to_col = lax.broadcasted_iota(jnp.int32, (columns, columns), 1)
    wanted = jnp.where(to_col < columns // 2, 2 * to_col, 2 * to_col - columns + 1)
    chosen = jnp.where(from_col == wanted, 1.0, 0.0).astype(jnp.bfloat16)
    for row in range(rf):
        split = jnp.dot(panel[row], chosen, preferred_element_type=jnp.float32)
        stacked = jnp.concatenate([split[:, :columns // 2], split[:, columns // 2:]], axis=0)
        lhs_ref[row] = jnp.transpose(stacked).astype(jnp.bfloat16)

    lane = lax.broadcasted_iota(jnp.int32, (tile, LANES), 1)
    lo = lane < tile

    def first_products(row, k):
        both = a_ref[row, :, k * tile:k * tile + LANES]
        none = jnp.zeros_like(both)
        left = jnp.concatenate([jnp.where(lo, both, none), jnp.where(lo, none, both)], axis=0)
        right = jnp.concatenate([panel[idx_ref[row, k]], panel[idx_ref[row, k + 1]]], axis=0)
        return jnp.dot(left, right, preferred_element_type=jnp.float32)

    def keep(u, y):
        for m in range(width // 2):
            x = y[:, m * LANES:(m + 1) * LANES]
            y_buf[u, :, 2 * m * LANES:(2 * m + 1) * LANES] = x.astype(jnp.bfloat16)
            y_buf[u, :, (2 * m + 1) * LANES:(2 * m + 2) * LANES] = pltpu.roll(x, tile, 1).astype(jnp.bfloat16)

    def second_product(row, u):
        lhs = lhs_ref[row]
        w = []
        for m in range(width // 2):
            x = y_buf[u, :, 2 * m * LANES:(2 * m + 1) * LANES]
            xr = y_buf[u, :, (2 * m + 1) * LANES:(2 * m + 2) * LANES]
            none = jnp.zeros_like(x)
            right = jnp.concatenate(
                [
                    jnp.concatenate([jnp.where(lo, x, none), jnp.where(lo, xr, none)], axis=1),
                    jnp.concatenate([jnp.where(lo, none, xr), jnp.where(lo, none, x)], axis=1),
                ],
                axis=0,
            )
            w.append(jnp.dot(lhs, right, preferred_element_type=jnp.float32))
        return w

    def add(row, k, w):
        for q in range(width):
            part = w[q // 2][:, q % 2 * LANES:(q % 2 + 1) * LANES]
            for s in range(0, width, ACCS):
                group = range(s, min(s + ACCS, width))
                places = [place_ref[row, (n * tiles + k) * width + q] for n in group]
                old = [acc[place] for acc, place in zip(accs, places)]
                for acc, place, was, n in zip(accs, places, old, group):
                    acc[place] = was + part[n * sub:(n + 1) * sub]

    def keep_two(u, y):
        keep(u, y[:tile])
        keep(u + 1, y[tile:])

    def hold(n, w):
        for m, part in enumerate(w):
            w_buf[n, :, m * 2 * LANES:(m + 1) * 2 * LANES] = part

    def held(n):
        return [w_buf[n, :, m * 2 * LANES:(m + 1) * 2 * LANES] for m in range(width // 2)]

    for k in range(0, tiles, 2):
        keep_two(k, first_products(0, k))
    for n in range(AHEAD):
        hold(n, second_product(0, n))

    def block_row(row, carry):
        following = jnp.minimum(row + 1, rf - 1)
        w = [held(n) for n in range(AHEAD)]
        for k in range(tiles):
            if k % 2 == 0:
                upcoming = first_products(following, k)
            ahead = k + AHEAD
            w.append(second_product(row, ahead) if ahead < tiles else second_product(following, ahead - tiles))
            add(row, k, w.pop(0))
            if k % 2 == 1:
                keep_two(k - 1, upcoming)
        for n in range(AHEAD):
            hold(n, w[n])
        return carry

    lax.fori_loop(0, rf, block_row, 0)

    named = jnp.zeros((NAME_ROWS, LANES), jnp.float32)
    here = lax.broadcasted_iota(jnp.int32, named.shape, 0)
    for n in range(groups * cap // LANES):
        part = names[:, n * LANES:(n + 1) * LANES]
        named = jnp.where(here == n, jnp.broadcast_to(part, named.shape), named)

    for (first, count), out in zip(spans, outs):

        def merge(c, carry):
            blocks = pl.ds(first + c * chunk, chunk)
            total = accs[0][blocks]
            for acc in accs[1:]:
                total = total + acc[blocks]
            rows = pl.ds(pl.multiple_of(c * (chunk * sub), chunk * sub), chunk * sub)
            out[rows, :] = total.reshape(chunk * sub, LANES).astype(out.dtype)
            return carry

        lax.fori_loop(0, count // chunk, merge, 0)
        out[count * sub:, :] = named.astype(out.dtype)


def partial_sums(ints, row_parts, pieces, table_of, tables, spans, groups, cap):
    rf, tile, cols = row_parts[0].shape
    sub = tile * tile // LANES
    width = pieces[0].shape[2]
    rows = sum(x.shape[0] for x in pieces)
    n_places = ints.shape[1] - cols // tile
    operands = [ints] + row_parts + pieces
    panel_bytes = rows * tile * width * 2
    return pl.pallas_call(
        functools.partial(partial_kernel, len(row_parts), len(pieces), spans, cap, groups, table_of),
        out_shape=[jax.ShapeDtypeStruct((n * sub + NAME_ROWS, LANES), jnp.bfloat16) for _, n in spans],
        grid_spec=pl.GridSpec(
            grid=(1,),
            in_specs=[pl.BlockSpec(memory_space=pl.ANY)] * len(operands),
            out_specs=[pl.BlockSpec((n * sub + NAME_ROWS, LANES), lambda i: (0, 0)) for _, n in spans],
            scratch_shapes=[pltpu.VMEM((tables * cap + 1, sub, LANES), jnp.float32)] * ACCS
            + [
                pltpu.VMEM((rf, tile, cols), jnp.bfloat16),
                pltpu.VMEM((rf, width // 2, 2 * tile), jnp.bfloat16),
                pltpu.VMEM((rows, tile, width), jnp.bfloat16),
                pltpu.VMEM((cols // tile, tile, 2 * width), jnp.bfloat16),
                pltpu.VMEM((AHEAD, width // 2, 2 * width), jnp.float32),
                pltpu.VMEM(ints.shape, jnp.int32),
                pltpu.VMEM((rf, n_places), jnp.int32),
                pltpu.VMEM((rf, LANES), jnp.int32),
                pltpu.SMEM((rf, n_places), jnp.int32),
                pltpu.SMEM((rf, LANES), jnp.int32),
                pltpu.SemaphoreType.DMA((len(operands) + 2,)),
            ],
        ),
        compiler_params=pltpu.CompilerParams(
            dimension_semantics=("arbitrary",), vmem_limit_bytes=26 * 1024 * 1024 + panel_bytes
        ),
        cost_estimate=pl.CostEstimate(flops=1, bytes_accessed=1, transcendentals=0),
        name="partial_sums",
    )(*operands)


def early_kernel(me_ref, *refs):
    tables, out_ref, accs, (vmem_names, smem_names, sem) = refs[:4], refs[4], refs[5:-3], refs[-3:]
    n_out, sub = out_ref.shape[:2]
    counts = [(x.shape[0] - NAME_ROWS) // sub for x in tables]
    cap, some = counts[0], counts[-1]
    chunk = 8
    at = me_ref[0] * cap
    row, lane = lax.div(at, jnp.int32(LANES)), lax.rem(at, jnp.int32(LANES))

    for n, (x, count) in enumerate(zip(tables, counts)):
        vmem_names[n] = x[pl.ds(count * sub, NAME_ROWS), :].astype(jnp.float32).astype(jnp.int32)
    copy = pltpu.make_async_copy(vmem_names, smem_names, sem)
    copy.start()

    def clear(c, carry):
        for acc in accs:
            acc[pl.ds(c * chunk, chunk)] = jnp.zeros((chunk, sub, LANES), jnp.float32)
        return carry

    lax.fori_loop(0, n_out // chunk, clear, 0)
    copy.wait()

    def add_to(c, numbers):
        src = pl.ds(pl.multiple_of(c * sub, sub), sub)
        names = [smem_names[n, row, lane + c] for n in numbers]
        old = [acc[name] for acc, name in zip(accs, names)]
        for acc, name, was, n in zip(accs, names, old, numbers):
            acc[name] = was + tables[n][src, :].astype(jnp.float32)

    def add(c, carry):
        add_to(c, (0, 1, 2))
        return carry

    def add_some(c, carry):
        add_to(c, (3,))
        return carry

    lax.fori_loop(0, cap, add, 0, unroll=4)
    lax.fori_loop(0, some, add_some, 0, unroll=4)

    def merge(c, carry):
        blocks = pl.ds(c * chunk, chunk)
        total = accs[0][blocks]
        for acc in accs[1:]:
            total = total + acc[blocks]
        out_ref[blocks] = total
        return carry

    lax.fori_loop(0, n_out // chunk, merge, 0)


def last_kernel(cap, me_ref, table, from_b, from_c, out_ref, acc, rows_buf, vmem_names, smem_names, sems):
    n_out, sub = acc.shape[:2]
    rest = (from_b.shape[0] - NAME_ROWS) // sub
    at, pick = me_ref[0] * cap, me_ref[1] == 1
    row, lane = lax.div(at, jnp.int32(LANES)), lax.rem(at, jnp.int32(LANES)) + (cap - rest)
    fill = pltpu.make_async_copy(table, acc, sems.at[0])
    fill.start()

    def arrived(rows):
        return jnp.where(pick, from_b[rows, :].astype(jnp.float32), from_c[rows, :].astype(jnp.float32))

    vmem_names[...] = arrived(pl.ds(rest * sub, NAME_ROWS)).astype(jnp.int32)
    copy = pltpu.make_async_copy(vmem_names, smem_names, sems.at[1])
    copy.start()
    copy.wait()
    fill.wait()

    def add(c, carry):
        acc[smem_names[row, lane + c]] += arrived(pl.ds(pl.multiple_of(c * sub, sub), sub))
        return carry

    lax.fori_loop(0, rest, add, 0, unroll=4)
    flat = acc.reshape(n_out * sub, LANES)

    def emit(c, carry):
        rows = pl.ds(pl.multiple_of(c * 8, 8), 8)
        for t in range(sub):
            rows_buf[rows, t * LANES:(t + 1) * LANES] = flat[pl.ds(c * (8 * sub) + t, 8, stride=sub), :]
        return carry

    parts = sems.shape[0] - 2
    height = n_out // parts
    copies = []
    for n in range(parts):
        lax.fori_loop(n * height // 8, (n + 1) * height // 8, emit, 0)
        rows = pl.ds(n * height, height)
        copies.append(pltpu.make_async_copy(rows_buf.at[rows], out_ref.at[rows], sems.at[2 + n]))
        copies[-1].start()
    for copy in copies:
        copy.wait()


def owner_sums(me, tables, last_b, last_c, cap, sub):
    def whole(x):
        return pl.BlockSpec(x.shape, lambda i, *_: (0,) * len(x.shape))

    table = jax.ShapeDtypeStruct((OSLOT, sub, LANES), jnp.float32)
    early = pl.pallas_call(
        early_kernel,
        out_shape=table,
        grid_spec=pltpu.PrefetchScalarGridSpec(
            num_scalar_prefetch=1,
            grid=(1,),
            in_specs=[whole(x) for x in tables],
            out_specs=whole(table),
            scratch_shapes=[pltpu.VMEM(table.shape, jnp.float32)] * (len(tables) - 1)
            + [
                pltpu.VMEM((len(tables), NAME_ROWS, LANES), jnp.int32),
                pltpu.SMEM((len(tables), NAME_ROWS, LANES), jnp.int32),
                pltpu.SemaphoreType.DMA,
            ],
        ),
        compiler_params=pltpu.CompilerParams(
            dimension_semantics=("arbitrary",), vmem_limit_bytes=20 * 1024 * 1024
        ),
        name="early_sums",
    )(me, *tables)
    return pl.pallas_call(
        functools.partial(last_kernel, cap),
        out_shape=jax.ShapeDtypeStruct((OSLOT, sub * LANES), jnp.float32),
        grid_spec=pltpu.PrefetchScalarGridSpec(
            num_scalar_prefetch=1,
            grid=(1,),
            in_specs=[pl.BlockSpec(memory_space=pl.ANY), whole(last_b), whole(last_c)],
            out_specs=pl.BlockSpec(memory_space=pl.ANY),
            scratch_shapes=[
                pltpu.VMEM(table.shape, jnp.float32),
                pltpu.VMEM((OSLOT, sub * LANES), jnp.float32),
                pltpu.VMEM((NAME_ROWS, LANES), jnp.int32),
                pltpu.SMEM((NAME_ROWS, LANES), jnp.int32),
                pltpu.SemaphoreType.DMA((2 + 4,)),
            ],
        ),
        compiler_params=pltpu.CompilerParams(
            dimension_semantics=("arbitrary",), vmem_limit_bytes=20 * 1024 * 1024
        ),
        name="owner_sums",
    )(me, early, last_b, last_c)


def swap(x, axis, d):
    return lax.ppermute(x, axis, [(i, i ^ d) for i in range(lax.axis_size(axis))])


def direct(p_tiles):
    return [swap(p_tiles, "blk", d) for d in range(2, lax.axis_size("blk"), 2)]


def body(a_tiles, a_cols, p_tiles, route_list, out_slot):
    groups = lax.axis_size("grp")
    me = lax.axis_index("grp")
    rf, tile, cols = a_tiles.shape
    cap = out_slot.shape[1] // groups
    sub = tile * tile // LANES
    middle = (me == 1) | (me == 2)
    takes = [(1, 0), (3, 1), (0, 2), (2, 3)]

    def take(x):
        return lax.ppermute(x, "grp", takes)

    ints = jnp.concatenate([route_list, a_cols], axis=1)
    ints = jnp.concatenate([ints, jnp.pad(out_slot, ((0, 0), (0, a_cols.shape[1])))], axis=0)
    ints_took = take(ints)
    far = direct(p_tiles)
    p_took = take(p_tiles)
    a_took = take(a_tiles)
    far[0], p_took = lax.optimization_barrier((far[0], p_took))
    far_took = direct(p_took)
    half = len(far) // 2
    mine = [jnp.concatenate([p_tiles] + far[:half]), jnp.concatenate(far[half:])]
    other = [swap(x, "blk", 1) for x in mine]

    def tables_own(off, middle):
        ends = jnp.where(off < 2, off, jnp.where(off == 3, 2, 3))
        return jnp.where(middle, jnp.where(off == 0, 0, jnp.where(off == 1, 3, off - 1)), ends)

    def tables_took(off, middle):
        return jnp.where((off == 0) | ((off == 1) & middle), off, 2)

    first = cap // 4
    spans = ((0, cap), (cap, cap), (2 * cap, first), (2 * cap + first, cap - first))
    own, to_a, to_b, last_b = partial_sums(
        ints, [a_tiles], mine + other, tables_own, 3, spans, groups, cap
    )
    own, a_took, ints_took, p_took, *far_took = lax.optimization_barrier((own, a_took, ints_took, p_took, *far_took))
    from_b = lax.ppermute(to_b, "grp", [(1, 2), (2, 1), (0, 3), (3, 0)])
    from_a = lax.ppermute(to_a, "grp", [(0, 1), (3, 2), (1, 3), (2, 0)])
    last_b = lax.ppermute(last_b, "grp", [(1, 2), (2, 1)])
    took = [p_took] + far_took
    pieces = took + [swap(x, "blk", 1) for x in took]
    spans = ((0, cap), (cap + first, cap - first))
    own_took, last_c = partial_sums(ints_took, [a_took], pieces, tables_took, 2, spans, groups, cap)
    own_took, last_c, from_b = lax.optimization_barrier((own_took, last_c, from_b))
    last_c = lax.ppermute(last_c, "grp", [(1, 0), (2, 3)])
    about = jnp.stack([me, middle.astype(me.dtype)])
    return owner_sums(about, [own, own_took, from_a, from_b], last_b, last_c, cap, sub)


def solution(mesh):
    in_specs = (
        P(("blk", "grp"), None, None),
        P(("blk", "grp"), None),
        P(("blk", "grp"), None, None),
        P(("blk", "grp"), None),
        P(("blk", "grp"), None),
    )
    out_specs = P(("blk", "grp"), None)
    return jax.shard_map(body, mesh=mesh, in_specs=in_specs, out_specs=out_specs, check_vma=False)
```

profile of v0, /device:TPU:0, one launch (start us, length us, event | category | flops | bytes accessed | tf_op | source)
XLA Modules:
  0.0 69.1 jit_solution(2245841306075602554)
XLA Ops:
  0.0 0.0 copy-start
  0.0 0.0 copy-start.2
  0.0 0.0 copy-start.1
  0.0 0.0 copy-start.3
  0.0 3.0 %collective-permute-start = (bf16[8,64,256]{2,1,0:T(8,128)(2,1)}, bf16[8,64,256]{2,1,0:T(8,128)(2,1)S(1)}, u32[]{:S(2)}, u32[]{:S(2)}) collective-permute-start(bf16[8,64,256]{2,1,0:T(8,128)(2,1)} %param.7), channel_id=1, source_target_pairs={{0,8},{4,12},{8,0},{12,4},{16,24},{20,28},{24,16},{28,20},{1,9},{5... | collective-permute-start | bytes 786440 | tf_op jit(solution)/shard_map/ppermute | solution.py:362
  3.0 2.6 %collective-permute-start.1 = (bf16[8,64,256]{2,1,0:T(8,128)(2,1)}, bf16[8,64,256]{2,1,0:T(8,128)(2,1)S(1)}, u32[]{:S(2)}, u32[]{:S(2)}) collective-permute-start(bf16[8,64,256]{2,1,0:T(8,128)(2,1)} %param.7), channel_id=1, source_target_pairs={{1,0},{3,1},{0,2},{2,3},{5,4},{7,5},{4,6},{6,7},{9,8},{11,9},{8,10... | collective-permute-start | bytes 786440 | tf_op jit(solution)/shard_map/ppermute | solution.py:379
  5.6 1.6 %collective-permute-start.6 = (bf16[8,64,1024]{2,1,0:T(8,128)(2,1)}, bf16[8,64,1024]{2,1,0:T(8,128)(2,1)S(1)}, u32[]{:S(2)}, u32[]{:S(2)}) collective-permute-start(bf16[8,64,1024]{2,1,0:T(8,128)(2,1)} %refs_0_.1), channel_id=1, source_target_pairs={{1,0},{3,1},{0,2},{2,3},{5,4},{7,5},{4,6},{6,7},{9,8},{11,9},{8,10... | collective-permute-start | bytes 3145736 | tf_op jit(solution)/shard_map/ppermute | solution.py:379
  7.2 1.5 %collective-permute-start.2 = (bf16[8,64,256]{2,1,0:T(8,128)(2,1)}, bf16[8,64,256]{2,1,0:T(8,128)(2,1)S(1)}, u32[]{:S(2)}, u32[]{:S(2)}) collective-permute-start(bf16[8,64,256]{2,1,0:T(8,128)(2,1)} %param.7), channel_id=1, source_target_pairs={{0,16},{4,20},{8,24},{12,28},{16,0},{20,4},{24,8},{28,12},{1,17},{... | collective-permute-start | bytes 786440 | tf_op jit(solution)/shard_map/ppermute | solution.py:362
  8.7 0.5 collective-permute-start.3
  9.2 1.0 %constant_dynamic-update-slice_fusion.1 = bf16[16,64,256]{2,1,0:T(8,128)(2,1)S(1)} fusion(bf16[8,64,256]{2,1,0:T(8,128)(2,1)} %param.7), kind=kLoop, calls=%fused_computation.2 | loop fusion | bytes 524288
  10.2 0.0 collective-permute-done
  10.2 2.5 %collective-permute-done.1.refs_1_ = bf16[8,64,256]{2,1,0:T(8,128)(2,1)S(1)} collective-permute-done((bf16[8,64,256]{2,1,0:T(8,128)(2,1)}, bf16[8,64,256]{2,1,0:T(8,128)(2,1)S(1)}, u32[]{:S(2)}, u32[]{:S(2)}) %collective-permute-start.1) | collective-permute-done | bytes 262176 | tf_op jit(solution)/shard_map/ppermute | solution.py:379
  12.7 0.1 collective-permute-start.4
  12.8 7.4 %collective-permute-done.2 = bf16[8,64,256]{2,1,0:T(8,128)(2,1)S(1)} collective-permute-done((bf16[8,64,256]{2,1,0:T(8,128)(2,1)}, bf16[8,64,256]{2,1,0:T(8,128)(2,1)S(1)}, u32[]{:S(2)}, u32[]{:S(2)}) %collective-permute-start.2) | collective-permute-done | bytes 262176 | tf_op jit(solution)/shard_map/ppermute | solution.py:362
  20.2 0.0 collective-permute-done.3
  20.3 0.1 collective-permute-start.5
  20.4 1.6 %collective-permute-start.10 = (bf16[8,64,256]{2,1,0:T(8,128)(2,1)S(1)}, bf16[8,64,256]{2,1,0:T(8,128)(2,1)S(1)}, u32[]{:S(2)}, u32[]{:S(2)}) collective-permute-start(bf16[8,64,256]{2,1,0:T(8,128)(2,1)S(1)} %collective-permute-done.1.refs_1_), channel_id=1, source_target_pairs={{0,24},{4,28},{8,16},{12,20},{16,8},{20,12},{24,0},{28,4},{1,25},{... | collective-permute-start | bytes 786440 | tf_op jit(solution)/shard_map/ppermute | solution.py:362
  21.9 1.5 %collective-permute-start.8 = (bf16[8,64,256]{2,1,0:T(8,128)(2,1)S(1)}, bf16[8,64,256]{2,1,0:T(8,128)(2,1)S(1)}, u32[]{:S(2)}, u32[]{:S(2)}) collective-permute-start(bf16[8,64,256]{2,1,0:T(8,128)(2,1)S(1)} %collective-permute-done.1.refs_1_), channel_id=1, source_target_pairs={{0,8},{4,12},{8,0},{12,4},{16,24},{20,28},{24,16},{28,20},{1,9},{5... | collective-permute-start | bytes 786440 | tf_op jit(solution)/shard_map/ppermute | solution.py:362
  23.4 0.0 collective-permute-done.4.refs_3_
  23.4 0.5 collective-permute-start.9
  23.9 0.0 copy-done.2
  23.9 0.0 copy-done.1
  23.9 0.0 copy-done.3
  23.9 0.0 collective-permute-done.5.refs_4_
  23.9 0.4 collective-permute-start.7
  24.3 0.0 copy-done
  24.3 9.6 %partial_sums.2 = (bf16[2064,128]{1,0:T(8,128)(2,1)S(1)}, bf16[2064,128]{1,0:T(8,128)(2,1)S(1)}, bf16[528,128]{1,0:T(8,128)(2,1)S(1)}, bf16[1552,128]{1,0:T(8,128)(2,1)S(1)}) custom-call(s32[9,272]{1,0:T(8,128)S(1)} %pad_add_fusion.ints, bf16[8,64,1024]{2,1,0:T(8,128)(2,1)S(1)} %copy-done, ...), custom_call_target="tpu_custom_call" | custom-call | flops 1 | bytes 1 | tf_op jit(solution)/shard_map/partial_sums/pallas_call | solution.py:190
  33.9 0.2 collective-permute-done.7.ints
  34.1 0.0 collective-permute-done.10.refs_4_
  34.1 1.6 %collective-permute-done.8.refs_2_ = bf16[8,64,256]{2,1,0:T(8,128)(2,1)S(1)} collective-permute-done((bf16[8,64,256]{2,1,0:T(8,128)(2,1)S(1)}, bf16[8,64,256]{2,1,0:T(8,128)(2,1)S(1)}, u32[]{:S(2)}, u32[]{:S(2)}) %collective-permute-start.8) | collective-permute-done | bytes 262176 | tf_op jit(solution)/shard_map/ppermute | solution.py:362
  35.7 0.0 collective-permute-done.9.refs_3_
  35.7 0.0 collective-permute-done.6.refs_0_
  35.7 0.0 collective-permute-start.11
  35.7 0.5 collective-permute-start.12
  36.2 0.1 collective-permute-start.13
  36.3 0.4 collective-permute-start.14
  36.7 2.0 %collective-permute-start.15 = (bf16[528,128]{1,0:T(8,128)(2,1)S(1)}, bf16[528,128]{1,0:T(8,128)(2,1)S(1)}, u32[]{:S(2)}, u32[]{:S(2)}) collective-permute-start(bf16[528,128]{1,0:T(8,128)(2,1)S(1)} %get-tuple-element.35), channel_id=1, source_target_pairs={{1,2},{2,1},{0,3},{3,0},{5,6},{6,5},{4,7},{7,4},{9,10},{10,9},{8,1... | collective-permute-start | bytes 405512 | tf_op jit(solution)/shard_map/ppermute | solution.py:406
  38.7 0.0 collective-permute-done.11.refs_5_
  38.7 0.5 collective-permute-start.16
  39.2 0.0 collective-permute-done.12.refs_6_
  39.2 0.7 collective-permute-start.17
  39.9 0.0 collective-permute-done.13.refs_7_
  39.9 0.0 collective-permute-done.14.refs_8_
  39.9 10.5 %partial_sums.3 = (bf16[2064,128]{1,0:T(8,128)(2,1)S(1)}, bf16[1552,128]{1,0:T(8,128)(2,1)}) custom-call(s32[9,272]{1,0:T(8,128)S(1)} %collective-permute-done.7.ints, bf16[8,64,1024]{2,1,0:T(8,128)(2,1)S(1)} %collective-permute-done.6.refs_0_, bf16[8,64,256]{2,1,0:T(8,128)(2,1)S(1)} %collective-permute-done.1.refs_1_, ...), custom_call_target="tpu_custom_call" | custom-call | flops 1 | bytes 1 | tf_op jit(solution)/shard_map/partial_sums/pallas_call | solution.py:190
  50.4 0.0 collective-permute-done.15.refs_3_
  50.4 1.3 %collective-permute-start.18 = (bf16[1552,128]{1,0:T(8,128)(2,1)}, bf16[1552,128]{1,0:T(8,128)(2,1)S(1)}, u32[]{:S(2)}, u32[]{:S(2)}) collective-permute-start(bf16[1552,128]{1,0:T(8,128)(2,1)} %get-tuple-element.40), channel_id=1, source_target_pairs={{1,0},{2,3},{5,4},{6,7},{9,8},{10,11},{13,12},{14,15},{17,16},{18,... | collective-permute-start | bytes 1191944 | tf_op jit(solution)/shard_map/ppermute | solution.py:414
  51.7 0.1 pad_add_fusion.1.me_ref
  51.8 5.9 %collective-permute-done.16.refs_2_ = bf16[2064,128]{1,0:T(8,128)(2,1)S(1)} collective-permute-done((bf16[2064,128]{1,0:T(8,128)(2,1)S(1)}, bf16[2064,128]{1,0:T(8,128)(2,1)S(1)}, u32[]{:S(2)}, u32[]{:S(2)}) %collective-permute-start.16) | collective-permute-done | bytes 528416 | tf_op jit(solution)/shard_map/ppermute | solution.py:407
  57.7 2.6 %early_sums.1.table = f32[128,32,128]{2,1,0:T(8,128)S(1)} custom-call(s32[2]{0:T(128)S(1)} %pad_add_fusion.1.me_ref, bf16[2064,128]{1,0:T(8,128)(2,1)S(1)} %get-tuple-element.26.refs_0_, bf16[2064,128]{1,0:T(8,128)(2,1)S(1)} %get-tuple-element.36.refs_1_, bf16[2064,128]{1,0:T(8,128)(2,1)S(1)} %collective-permute-done.16.refs_2_, ...), custom_call_target="tpu_custom_call" | custom-call | tf_op jit(solution)/shard_map/early_sums/pallas_call | solution.py:318
  60.3 0.0 collective-permute-done.17.from_b
  60.3 5.0 %collective-permute-done.18.from_c = bf16[1552,128]{1,0:T(8,128)(2,1)S(1)} collective-permute-done((bf16[1552,128]{1,0:T(8,128)(2,1)}, bf16[1552,128]{1,0:T(8,128)(2,1)S(1)}, u32[]{:S(2)}, u32[]{:S(2)}) %collective-permute-start.18) | collective-permute-done | bytes 397344 | tf_op jit(solution)/shard_map/ppermute | solution.py:414
  65.3 3.8 %owner_sums.1 = f32[128,4096]{1,0:T(8,128)} custom-call(s32[2]{0:T(128)S(1)} %pad_add_fusion.1.me_ref, f32[128,32,128]{2,1,0:T(8,128)S(1)} %early_sums.1.table, bf16[1552,128]{1,0:T(8,128)(2,1)S(1)} %collective-permute-done.17.from_b, bf16[1552,128]{1,0:T(8,128)(2,1)S(1)} %collective-permute-done.18.from_c), custom_call_target="tpu_custom_call" | custom-call | tf_op jit(solution)/shard_map/owner_sums/pallas_call | solution.py:338
  (4 shorter events, 0.1 us)
Async XLA Ops:
  0.0 24.3 %copy-start = (bf16[8,64,1024]{2,1,0:T(8,128)(2,1)S(1)}, bf16[8,64,1024]{2,1,0:T(8,128)(2,1)}, u32[]{:S(2)}) copy-start(bf16[8,64,1024]{2,1,0:T(8,128)(2,1)} %refs_0_.1) | copy-start | bytes 3145732
  0.0 23.9 %copy-start.2 = (s32[8,16]{1,0:T(8,128)S(1)}, s32[8,16]{1,0:T(8,128)}, u32[]{:S(2)}) copy-start(s32[8,16]{1,0:T(8,128)} %param.6) | copy-start | bytes 1540
  0.0 23.9 %copy-start.1 = (s32[8,256]{1,0:T(8,128)S(1)}, s32[8,256]{1,0:T(8,128)}, u32[]{:S(2)}) copy-start(s32[8,256]{1,0:T(8,128)} %param.8) | copy-start | bytes 24580
  0.0 23.9 %copy-start.3 = (s32[1,256]{1,0:T(1,128)S(1)}, s32[1,256]{1,0:T(1,128)}, u32[]{:S(2)}) copy-start(s32[1,256]{1,0:T(1,128)} %param.9) | copy-start | bytes 3076
  0.0 10.2 %collective-permute-start = (bf16[8,64,256]{2,1,0:T(8,128)(2,1)}, bf16[8,64,256]{2,1,0:T(8,128)(2,1)S(1)}, u32[]{:S(2)}, u32[]{:S(2)}) collective-permute-start(bf16[8,64,256]{2,1,0:T(8,128)(2,1)} %param.7), channel_id=1, source_target_pairs={{0,8},{4,12},{8,0},{12,4},{16,24},{20,28},{24,16},{28,20},{1,9},{5... | collective-permute-start | bytes 786440 | tf_op jit(solution)/shard_map/ppermute | solution.py:362
  3.0 9.7 %collective-permute-start.1 = (bf16[8,64,256]{2,1,0:T(8,128)(2,1)}, bf16[8,64,256]{2,1,0:T(8,128)(2,1)S(1)}, u32[]{:S(2)}, u32[]{:S(2)}) collective-permute-start(bf16[8,64,256]{2,1,0:T(8,128)(2,1)} %param.7), channel_id=1, source_target_pairs={{1,0},{3,1},{0,2},{2,3},{5,4},{7,5},{4,6},{6,7},{9,8},{11,9},{8,10... | collective-permute-start | bytes 786440 | tf_op jit(solution)/shard_map/ppermute | solution.py:379
  5.6 30.1 %collective-permute-start.6 = (bf16[8,64,1024]{2,1,0:T(8,128)(2,1)}, bf16[8,64,1024]{2,1,0:T(8,128)(2,1)S(1)}, u32[]{:S(2)}, u32[]{:S(2)}) collective-permute-start(bf16[8,64,1024]{2,1,0:T(8,128)(2,1)} %refs_0_.1), channel_id=1, source_target_pairs={{1,0},{3,1},{0,2},{2,3},{5,4},{7,5},{4,6},{6,7},{9,8},{11,9},{8,10... | collective-permute-start | bytes 3145736 | tf_op jit(solution)/shard_map/ppermute | solution.py:379
  7.2 13.0 %collective-permute-start.2 = (bf16[8,64,256]{2,1,0:T(8,128)(2,1)}, bf16[8,64,256]{2,1,0:T(8,128)(2,1)S(1)}, u32[]{:S(2)}, u32[]{:S(2)}) collective-permute-start(bf16[8,64,256]{2,1,0:T(8,128)(2,1)} %param.7), channel_id=1, source_target_pairs={{0,16},{4,20},{8,24},{12,28},{16,0},{20,4},{24,8},{28,12},{1,17},{... | collective-permute-start | bytes 786440 | tf_op jit(solution)/shard_map/ppermute | solution.py:362
  8.7 11.5 %collective-permute-start.3 = (bf16[8,64,256]{2,1,0:T(8,128)(2,1)}, bf16[8,64,256]{2,1,0:T(8,128)(2,1)S(1)}, u32[]{:S(2)}, u32[]{:S(2)}) collective-permute-start(bf16[8,64,256]{2,1,0:T(8,128)(2,1)} %param.7), channel_id=1, source_target_pairs={{0,24},{4,28},{8,16},{12,20},{16,8},{20,12},{24,0},{28,4},{1,25},{... | collective-permute-start | bytes 786440 | tf_op jit(solution)/shard_map/ppermute | solution.py:362
  12.7 10.7 %collective-permute-start.4 = (bf16[16,64,256]{2,1,0:T(8,128)(2,1)S(1)}, bf16[16,64,256]{2,1,0:T(8,128)(2,1)S(1)}, u32[]{:S(2)}, u32[]{:S(2)}) collective-permute-start(bf16[16,64,256]{2,1,0:T(8,128)(2,1)S(1)} %constant_dynamic-update-slice_fusion.refs_1_), channel_id=1, source_target_pairs={{0,4},{4,0},{8,12},{12,8},{16,20},{20,16},{24,28},{28,24},{1,5},{5... | collective-permute-start | bytes 1572872 | tf_op jit(solution)/shard_map/ppermute | solution.py:362
  20.3 3.7 %collective-permute-start.5 = (bf16[16,64,256]{2,1,0:T(8,128)(2,1)S(1)}, bf16[16,64,256]{2,1,0:T(8,128)(2,1)S(1)}, u32[]{:S(2)}, u32[]{:S(2)}) collective-permute-start(bf16[16,64,256]{2,1,0:T(8,128)(2,1)S(1)} %constant_dynamic-update-slice_fusion.2.refs_2_), channel_id=1, source_target_pairs={{0,4},{4,0},{8,12},{12,8},{16,20},{20,16},{24,28},{28,24},{1,5},{5... | collective-permute-start | bytes 1572872 | tf_op jit(solution)/shard_map/ppermute | solution.py:362
  20.4 13.7 %collective-permute-start.10 = (bf16[8,64,256]{2,1,0:T(8,128)(2,1)S(1)}, bf16[8,64,256]{2,1,0:T(8,128)(2,1)S(1)}, u32[]{:S(2)}, u32[]{:S(2)}) collective-permute-start(bf16[8,64,256]{2,1,0:T(8,128)(2,1)S(1)} %collective-permute-done.1.refs_1_), channel_id=1, source_target_pairs={{0,24},{4,28},{8,16},{12,20},{16,8},{20,12},{24,0},{28,4},{1,25},{... | collective-permute-start | bytes 786440 | tf_op jit(solution)/shard_map/ppermute | solution.py:362
  21.9 13.8 %collective-permute-start.8 = (bf16[8,64,256]{2,1,0:T(8,128)(2,1)S(1)}, bf16[8,64,256]{2,1,0:T(8,128)(2,1)S(1)}, u32[]{:S(2)}, u32[]{:S(2)}) collective-permute-start(bf16[8,64,256]{2,1,0:T(8,128)(2,1)S(1)} %collective-permute-done.1.refs_1_), channel_id=1, source_target_pairs={{0,8},{4,12},{8,0},{12,4},{16,24},{20,28},{24,16},{28,20},{1,9},{5... | collective-permute-start | bytes 786440 | tf_op jit(solution)/shard_map/ppermute | solution.py:362
  23.4 12.3 %collective-permute-start.9 = (bf16[8,64,256]{2,1,0:T(8,128)(2,1)S(1)}, bf16[8,64,256]{2,1,0:T(8,128)(2,1)S(1)}, u32[]{:S(2)}, u32[]{:S(2)}) collective-permute-start(bf16[8,64,256]{2,1,0:T(8,128)(2,1)S(1)} %collective-permute-done.1.refs_1_), channel_id=1, source_target_pairs={{0,16},{4,20},{8,24},{12,28},{16,0},{20,4},{24,8},{28,12},{1,17},{... | collective-permute-start | bytes 786440 | tf_op jit(solution)/shard_map/ppermute | solution.py:362
  23.9 10.2 %collective-permute-start.7 = (s32[9,272]{1,0:T(8,128)S(1)}, s32[9,272]{1,0:T(8,128)S(1)}, u32[]{:S(2)}, u32[]{:S(2)}) collective-permute-start(s32[9,272]{1,0:T(8,128)S(1)} %pad_add_fusion.ints), channel_id=1, source_target_pairs={{1,0},{3,1},{0,2},{2,3},{5,4},{7,5},{4,6},{6,7},{9,8},{11,9},{8,10... | collective-permute-start | bytes 29384 | tf_op jit(solution)/shard_map/ppermute | solution.py:379
  35.7 3.0 %collective-permute-start.11 = (bf16[8,64,256]{2,1,0:T(8,128)(2,1)S(1)}, bf16[8,64,256]{2,1,0:T(8,128)(2,1)S(1)}, u32[]{:S(2)}, u32[]{:S(2)}) collective-permute-start(bf16[8,64,256]{2,1,0:T(8,128)(2,1)S(1)} %collective-permute-done.1.refs_1_), channel_id=1, source_target_pairs={{0,4},{4,0},{8,12},{12,8},{16,20},{20,16},{24,28},{28,24},{1,5},{5... | collective-permute-start | bytes 786440 | tf_op jit(solution)/shard_map/ppermute | solution.py:362
  35.7 3.4 %collective-permute-start.12 = (bf16[8,64,256]{2,1,0:T(8,128)(2,1)S(1)}, bf16[8,64,256]{2,1,0:T(8,128)(2,1)S(1)}, u32[]{:S(2)}, u32[]{:S(2)}) collective-permute-start(bf16[8,64,256]{2,1,0:T(8,128)(2,1)S(1)} %collective-permute-done.8.refs_2_), channel_id=1, source_target_pairs={{0,4},{4,0},{8,12},{12,8},{16,20},{20,16},{24,28},{28,24},{1,5},{5... | collective-permute-start | bytes 786440 | tf_op jit(solution)/shard_map/ppermute | solution.py:362
  36.2 3.6 %collective-permute-start.13 = (bf16[8,64,256]{2,1,0:T(8,128)(2,1)S(1)}, bf16[8,64,256]{2,1,0:T(8,128)(2,1)S(1)}, u32[]{:S(2)}, u32[]{:S(2)}) collective-permute-start(bf16[8,64,256]{2,1,0:T(8,128)(2,1)S(1)} %collective-permute-done.9.refs_3_), channel_id=1, source_target_pairs={{0,4},{4,0},{8,12},{12,8},{16,20},{20,16},{24,28},{28,24},{1,5},{5... | collective-permute-start | bytes 786440 | tf_op jit(solution)/shard_map/ppermute | solution.py:362
  36.3 3.6 %collective-permute-start.14 = (bf16[8,64,256]{2,1,0:T(8,128)(2,1)S(1)}, bf16[8,64,256]{2,1,0:T(8,128)(2,1)S(1)}, u32[]{:S(2)}, u32[]{:S(2)}) collective-permute-start(bf16[8,64,256]{2,1,0:T(8,128)(2,1)S(1)} %collective-permute-done.10.refs_4_), channel_id=1, source_target_pairs={{0,4},{4,0},{8,12},{12,8},{16,20},{20,16},{24,28},{28,24},{1,5},{5... | collective-permute-start | bytes 786440 | tf_op jit(solution)/shard_map/ppermute | solution.py:362
  36.7 13.7 %collective-permute-start.15 = (bf16[528,128]{1,0:T(8,128)(2,1)S(1)}, bf16[528,128]{1,0:T(8,128)(2,1)S(1)}, u32[]{:S(2)}, u32[]{:S(2)}) collective-permute-start(bf16[528,128]{1,0:T(8,128)(2,1)S(1)} %get-tuple-element.35), channel_id=1, source_target_pairs={{1,2},{2,1},{0,3},{3,0},{5,6},{6,5},{4,7},{7,4},{9,10},{10,9},{8,1... | collective-permute-start | bytes 405512 | tf_op jit(solution)/shard_map/ppermute | solution.py:406
  38.7 19.0 %collective-permute-start.16 = (bf16[2064,128]{1,0:T(8,128)(2,1)S(1)}, bf16[2064,128]{1,0:T(8,128)(2,1)S(1)}, u32[]{:S(2)}, u32[]{:S(2)}) collective-permute-start(bf16[2064,128]{1,0:T(8,128)(2,1)S(1)} %get-tuple-element.37), channel_id=1, source_target_pairs={{0,1},{3,2},{1,3},{2,0},{4,5},{7,6},{5,7},{6,4},{8,9},{11,10},{9,1... | collective-permute-start | bytes 1585160 | tf_op jit(solution)/shard_map/ppermute | solution.py:407
  39.2 21.1 %collective-permute-start.17 = (bf16[1552,128]{1,0:T(8,128)(2,1)S(1)}, bf16[1552,128]{1,0:T(8,128)(2,1)S(1)}, u32[]{:S(2)}, u32[]{:S(2)}) collective-permute-start(bf16[1552,128]{1,0:T(8,128)(2,1)S(1)} %get-tuple-element.39), channel_id=1, source_target_pairs={{1,2},{2,1},{5,6},{6,5},{9,10},{10,9},{13,14},{14,13},{17,18},{18,... | collective-permute-start | bytes 1191944 | tf_op jit(solution)/shard_map/ppermute | solution.py:408
  50.4 14.9 %collective-permute-start.18 = (bf16[1552,128]{1,0:T(8,128)(2,1)}, bf16[1552,128]{1,0:T(8,128)(2,1)S(1)}, u32[]{:S(2)}, u32[]{:S(2)}) collective-permute-start(bf16[1552,128]{1,0:T(8,128)(2,1)} %get-tuple-element.40), channel_id=1, source_target_pairs={{1,0},{2,3},{5,4},{6,7},{9,8},{10,11},{13,12},{14,15},{17,16},{18,... | collective-permute-start | bytes 1191944 | tf_op jit(solution)/shard_map/ppermute | solution.py:414
where the time goes:
time: 69.3 us; the launch traced here: 69.1 us
  Pallas kernels  26.5 us (38%)
  waiting for transfers between devices  22.7 us (33%)
  starting transfers between devices  18.7 us (27%)
  local copies, waits for them, and re-layouts  1.07 us (2%)
    pallas_call x2, Pallas kernels, partial_sums(): pl.pallas_call(functools.partial(partial_kernel, len(row_parts), len(piec...  20.1 us
    ppermute x12, starting transfers between devices, swap(): lax.ppermute(x, axis, [(i, i ^ d) for i in range(lax.axis_size(axis))])  9.72 us
    ppermute x12, waiting for transfers between devices, swap(): lax.ppermute(x, axis, [(i, i ^ d) for i in range(lax.axis_size(axis))])  9.07 us
    ppermute x1, waiting for transfers between devices, body(): from_a = lax.ppermute(to_a, 'grp', [(0, 1), (3, 2), (1, 3), (2, 0)])  5.91 us
    ppermute x1, waiting for transfers between devices, body(): last_c = lax.ppermute(last_c, 'grp', [(1, 0), (2, 3)])  5.04 us
    ppermute x3, starting transfers between devices, take(): return lax.ppermute(x, 'grp', takes)  4.55 us
    pallas_call x1, Pallas kernels, owner_sums(): pl.pallas_call(functools.partial(last_kernel, cap), out_shape=jax.ShapeDt...  3.8 us
    ppermute x3, waiting for transfers between devices, take(): return lax.ppermute(x, 'grp', takes)  2.65 us
  transfers between devices with their start and end apart: 19, of which 6 were waited for; matrix products, arithmetic and copies ran while one was open for 2% of the time, Pallas kernels for 33%

commit v1 on v0

--- a/solution.py
+++ b/solution.py
@@ -268,28 +268,34 @@
     lax.fori_loop(0, n_out // chunk, merge, 0)
 
 
-def last_kernel(cap, me_ref, table, from_b, from_c, out_ref, acc, rows_buf, vmem_names, smem_names, sems):
+def last_kernel(me_ref, table, from_b, from_c, out_ref, acc, rows_buf, vmem_names, smem_names, sems):
     n_out, sub = acc.shape[:2]
-    rest = (from_b.shape[0] - NAME_ROWS) // sub
-    at, pick = me_ref[0] * cap, me_ref[1] == 1
-    row, lane = lax.div(at, jnp.int32(LANES)), lax.rem(at, jnp.int32(LANES)) + (cap - rest)
+    cap, rest = [(x.shape[0] - NAME_ROWS) // sub for x in (from_b, from_c)]
+    pick = me_ref[1] == 1
+    count = jnp.where(pick, cap, rest)
+    at = me_ref[0] * cap
+    row, lane = lax.div(at, jnp.int32(LANES)), lax.rem(at, jnp.int32(LANES)) + (cap - count)
     fill = pltpu.make_async_copy(table, acc, sems.at[0])
     fill.start()
 
-    def arrived(rows):
-        return jnp.where(pick, from_b[rows, :].astype(jnp.float32), from_c[rows, :].astype(jnp.float32))
-
-    vmem_names[...] = arrived(pl.ds(rest * sub, NAME_ROWS)).astype(jnp.int32)
+    def arrived(rows_b, rows_c):
+        return jnp.where(pick, from_b[rows_b, :].astype(jnp.float32), from_c[rows_c, :].astype(jnp.float32))
+
+    vmem_names[...] = arrived(pl.ds(cap * sub, NAME_ROWS), pl.ds(rest * sub, NAME_ROWS)).astype(jnp.int32)
     copy = pltpu.make_async_copy(vmem_names, smem_names, sems.at[1])
     copy.start()
     copy.wait()
     fill.wait()
 
     def add(c, carry):
-        acc[smem_names[row, lane + c]] += arrived(pl.ds(pl.multiple_of(c * sub, sub), sub))
-        return carry
-
-    lax.fori_loop(0, rest, add, 0, unroll=4)
+        for u in range(4):
+            n = c * 4 + u
+            rows_b = pl.ds(pl.multiple_of(n * sub, sub), sub)
+            rows_c = pl.ds(pl.multiple_of(jnp.minimum(n, rest - 1) * sub, sub), sub)
+            acc[smem_names[row, lane + n]] += arrived(rows_b, rows_c)
+        return carry
+
+    lax.fori_loop(0, lax.div(count, jnp.int32(4)), add, 0)
     flat = acc.reshape(n_out * sub, LANES)
 
     def emit(c, carry):
@@ -310,7 +316,7 @@
         copy.wait()
 
 
-def owner_sums(me, tables, last_b, last_c, cap, sub):
+def owner_sums(me, tables, from_b, from_c, sub):
     def whole(x):
         return pl.BlockSpec(x.shape, lambda i, *_: (0,) * len(x.shape))
 
@@ -336,12 +342,12 @@
         name="early_sums",
     )(me, *tables)
     return pl.pallas_call(
-        functools.partial(last_kernel, cap),
+        last_kernel,
         out_shape=jax.ShapeDtypeStruct((OSLOT, sub * LANES), jnp.float32),
         grid_spec=pltpu.PrefetchScalarGridSpec(
             num_scalar_prefetch=1,
             grid=(1,),
-            in_specs=[pl.BlockSpec(memory_space=pl.ANY), whole(last_b), whole(last_c)],
+            in_specs=[pl.BlockSpec(memory_space=pl.ANY), whole(from_b), whole(from_c)],
             out_specs=pl.BlockSpec(memory_space=pl.ANY),
             scratch_shapes=[
                 pltpu.VMEM(table.shape, jnp.float32),
@@ -355,7 +361,7 @@
             dimension_semantics=("arbitrary",), vmem_limit_bytes=20 * 1024 * 1024
         ),
         name="owner_sums",
-    )(me, early, last_b, last_c)
+    )(me, early, from_b, from_c)
 
 
 def swap(x, axis, d):
@@ -386,8 +392,7 @@
     a_took = take(a_tiles)
     far[0], p_took = lax.optimization_barrier((far[0], p_took))
     far_took = direct(p_took)
-    half = len(far) // 2
-    mine = [jnp.concatenate([p_tiles] + far[:half]), jnp.concatenate(far[half:])]
+    mine = [p_tiles, jnp.concatenate(far)]
     other = [swap(x, "blk", 1) for x in mine]
 
     def tables_own(off, middle):
@@ -398,22 +403,20 @@
         return jnp.where((off == 0) | ((off == 1) & middle), off, 2)
 
     first = cap // 4
-    spans = ((0, cap), (cap, cap), (2 * cap, first), (2 * cap + first, cap - first))
-    own, to_a, to_b, last_b = partial_sums(
-        ints, [a_tiles], mine + other, tables_own, 3, spans, groups, cap
-    )
+    spans = ((0, cap), (cap, cap), (2 * cap, cap), (2 * cap, first))
+    own, to_a, to_b, to_d = partial_sums(ints, [a_tiles], mine + other, tables_own, 3, spans, groups, cap)
     own, a_took, ints_took, p_took, *far_took = lax.optimization_barrier((own, a_took, ints_took, p_took, *far_took))
-    from_b = lax.ppermute(to_b, "grp", [(1, 2), (2, 1), (0, 3), (3, 0)])
+    from_d = lax.ppermute(to_d, "grp", [(0, 3), (3, 0)])
     from_a = lax.ppermute(to_a, "grp", [(0, 1), (3, 2), (1, 3), (2, 0)])
-    last_b = lax.ppermute(last_b, "grp", [(1, 2), (2, 1)])
+    from_b = lax.ppermute(to_b, "grp", [(1, 2), (2, 1)])
     took = [p_took] + far_took
     pieces = took + [swap(x, "blk", 1) for x in took]
     spans = ((0, cap), (cap + first, cap - first))
-    own_took, last_c = partial_sums(ints_took, [a_took], pieces, tables_took, 2, spans, groups, cap)
-    own_took, last_c, from_b = lax.optimization_barrier((own_took, last_c, from_b))
-    last_c = lax.ppermute(last_c, "grp", [(1, 0), (2, 3)])
+    own_took, to_c = partial_sums(ints_took, [a_took], pieces, tables_took, 2, spans, groups, cap)
+    own_took, to_c, from_d = lax.optimization_barrier((own_took, to_c, from_d))
+    from_c = lax.ppermute(to_c, "grp", [(1, 0), (2, 3)])
     about = jnp.stack([me, middle.astype(me.dtype)])
-    return owner_sums(about, [own, own_took, from_a, from_b], last_b, last_c, cap, sub)
+    return owner_sums(about, [own, own_took, from_a, from_d], from_b, from_c, sub)
 
 
 def solution(mesh):

time: 69.3 us -> 71.5 us (1.032)
  starting transfers between devices: 18.7 us -> 20.6 us
  waiting for transfers between devices: 22.7 us -> 21.1 us
  Pallas kernels: 26.5 us -> 27.4 us
  other arithmetic: 0.08 us -> 0.81 us
    ppermute x12, waiting for transfers between devices: 9.07 us -> 7.2 us  [swap(): lax.ppermute(x, axis, [(i, i ^ d) for i in range(lax.axis_size(axis))])]
    ppermute x3, starting transfers between devices: 4.55 us -> 5.78 us  [take(): return lax.ppermute(x, 'grp', takes)]
    pallas_call x2, Pallas kernels: 20.1 us -> 21 us  [partial_sums(): pl.pallas_call(functools.partial(partial_kernel, len(row_parts), len(piec...]
    ppermute x12, starting transfers between devices: 9.72 us -> 10.5 us  [swap(): lax.ppermute(x, axis, [(i, i ^ d) for i in range(lax.axis_size(axis))])]
    concatenate x1, other arithmetic: 0.01 us -> 0.73 us  [body(): jnp.concatenate([ints, jnp.pad(out_slot, ((0, 0), (0, a_cols.shape[1])))]...]
  transfers between devices with their start and end apart: 19 -> 19, of which waited for: 6 -> 5; matrix products, arithmetic and copies ran while one was open for 2% -> 1% of each run, Pallas kernels for 33% -> 33%
where the time goes in v1:
time: 71.5 us; the launch traced here: 71.1 us
  Pallas kernels  27.4 us (38%)
  waiting for transfers between devices  21.1 us (30%)
  starting transfers between devices  20.6 us (29%)
  local copies, waits for them, and re-layouts  1.01 us (1%)
  other arithmetic  0.81 us (1%)
    pallas_call x2, Pallas kernels, partial_sums(): pl.pallas_call(functools.partial(partial_kernel, len(row_parts), len(piec...  21 us
    ppermute x12, starting transfers between devices, swap(): lax.ppermute(x, axis, [(i, i ^ d) for i in range(lax.axis_size(axis))])  10.5 us
    ppermute x12, waiting for transfers between devices, swap(): lax.ppermute(x, axis, [(i, i ^ d) for i in range(lax.axis_size(axis))])  7.2 us
    ppermute x3, starting transfers between devices, take(): return lax.ppermute(x, 'grp', takes)  5.78 us
    ppermute x1, waiting for transfers between devices, body(): from_c = lax.ppermute(to_c, 'grp', [(1, 0), (2, 3)])  5.75 us
    ppermute x1, waiting for transfers between devices, body(): from_a = lax.ppermute(to_a, 'grp', [(0, 1), (3, 2), (1, 3), (2, 0)])  5.6 us
    pallas_call x1, Pallas kernels, owner_sums(): pl.pallas_call(last_kernel, out_shape=jax.ShapeDtypeStruct((OSLOT, sub *...  3.84 us
    pallas_call x1, Pallas kernels, owner_sums(): pl.pallas_call(early_kernel, out_shape=table, grid_spec=pltpu.PrefetchSca...  2.59 us
  transfers between devices with their start and end apart: 19, of which 5 were waited for; matrix products, arithmetic and copies ran while one was open for 1% of the time, Pallas kernels for 33%

profile of v1, /device:TPU:0, one launch (start us, length us, event | category | flops | bytes accessed | tf_op | source)
XLA Modules:
  0.0 71.1 jit_solution(10415698720746247639)
XLA Ops:
  0.0 0.0 copy-start
  0.0 2.9 %collective-permute-start = (bf16[8,64,256]{2,1,0:T(8,128)(2,1)}, bf16[8,64,256]{2,1,0:T(8,128)(2,1)S(1)}, u32[]{:S(2)}, u32[]{:S(2)}) collective-permute-start(bf16[8,64,256]{2,1,0:T(8,128)(2,1)} %refs_1_.1), channel_id=1, source_target_pairs={{0,8},{4,12},{8,0},{12,4},{16,24},{20,28},{24,16},{28,20},{1,9},{5... | collective-permute-start | bytes 786440 | tf_op jit(solution)/shard_map/ppermute | solution.py:368
  2.9 2.6 %collective-permute-start.1 = (bf16[8,64,256]{2,1,0:T(8,128)(2,1)}, bf16[8,64,256]{2,1,0:T(8,128)(2,1)S(1)}, u32[]{:S(2)}, u32[]{:S(2)}) collective-permute-start(bf16[8,64,256]{2,1,0:T(8,128)(2,1)} %refs_1_.1), channel_id=1, source_target_pairs={{1,0},{3,1},{0,2},{2,3},{5,4},{7,5},{4,6},{6,7},{9,8},{11,9},{8,10... | collective-permute-start | bytes 786440 | tf_op jit(solution)/shard_map/ppermute | solution.py:385
  5.5 1.5 %collective-permute-start.2 = (bf16[8,64,256]{2,1,0:T(8,128)(2,1)}, bf16[8,64,256]{2,1,0:T(8,128)(2,1)S(1)}, u32[]{:S(2)}, u32[]{:S(2)}) collective-permute-start(bf16[8,64,256]{2,1,0:T(8,128)(2,1)} %refs_1_.1), channel_id=1, source_target_pairs={{0,16},{4,20},{8,24},{12,28},{16,0},{20,4},{24,8},{28,12},{1,17},{... | collective-permute-start | bytes 786440 | tf_op jit(solution)/shard_map/ppermute | solution.py:368
  7.1 0.5 collective-permute-start.3
  7.5 1.6 %collective-permute-start.6 = (bf16[8,64,1024]{2,1,0:T(8,128)(2,1)}, bf16[8,64,1024]{2,1,0:T(8,128)(2,1)S(1)}, u32[]{:S(2)}, u32[]{:S(2)}) collective-permute-start(bf16[8,64,1024]{2,1,0:T(8,128)(2,1)} %refs_0_.1), channel_id=1, source_target_pairs={{1,0},{3,1},{0,2},{2,3},{5,4},{7,5},{4,6},{6,7},{9,8},{11,9},{8,10... | collective-permute-start | bytes 3145736 | tf_op jit(solution)/shard_map/ppermute | solution.py:385
  9.1 0.9 %collective-permute-done = bf16[8,64,256]{2,1,0:T(8,128)(2,1)S(1)} collective-permute-done((bf16[8,64,256]{2,1,0:T(8,128)(2,1)}, bf16[8,64,256]{2,1,0:T(8,128)(2,1)S(1)}, u32[]{:S(2)}, u32[]{:S(2)}) %collective-permute-start) | collective-permute-done | bytes 262176 | tf_op jit(solution)/shard_map/ppermute | solution.py:368
  10.0 2.5 %collective-permute-done.1.refs_1_ = bf16[8,64,256]{2,1,0:T(8,128)(2,1)S(1)} collective-permute-done((bf16[8,64,256]{2,1,0:T(8,128)(2,1)}, bf16[8,64,256]{2,1,0:T(8,128)(2,1)S(1)}, u32[]{:S(2)}, u32[]{:S(2)}) %collective-permute-start.1) | collective-permute-done | bytes 262176 | tf_op jit(solution)/shard_map/ppermute | solution.py:385
  12.6 6.2 %collective-permute-done.2 = bf16[8,64,256]{2,1,0:T(8,128)(2,1)S(1)} collective-permute-done((bf16[8,64,256]{2,1,0:T(8,128)(2,1)}, bf16[8,64,256]{2,1,0:T(8,128)(2,1)S(1)}, u32[]{:S(2)}, u32[]{:S(2)}) %collective-permute-start.2) | collective-permute-done | bytes 262176 | tf_op jit(solution)/shard_map/ppermute | solution.py:368
  18.9 0.0 collective-permute-done.3
  18.9 0.1 collective-permute-start.5
  19.0 0.5 collective-permute-start.4
  19.5 1.5 %collective-permute-start.10 = (bf16[8,64,256]{2,1,0:T(8,128)(2,1)S(1)}, bf16[8,64,256]{2,1,0:T(8,128)(2,1)S(1)}, u32[]{:S(2)}, u32[]{:S(2)}) collective-permute-start(bf16[8,64,256]{2,1,0:T(8,128)(2,1)S(1)} %collective-permute-done.1.refs_1_), channel_id=1, source_target_pairs={{0,24},{4,28},{8,16},{12,20},{16,8},{20,12},{24,0},{28,4},{1,25},{... | collective-permute-start | bytes 786440 | tf_op jit(solution)/shard_map/ppermute | solution.py:368
  21.0 1.5 %collective-permute-start.8 = (bf16[8,64,256]{2,1,0:T(8,128)(2,1)S(1)}, bf16[8,64,256]{2,1,0:T(8,128)(2,1)S(1)}, u32[]{:S(2)}, u32[]{:S(2)}) collective-permute-start(bf16[8,64,256]{2,1,0:T(8,128)(2,1)S(1)} %collective-permute-done.1.refs_1_), channel_id=1, source_target_pairs={{0,8},{4,12},{8,0},{12,4},{16,24},{20,28},{24,16},{28,20},{1,9},{5... | collective-permute-start | bytes 786440 | tf_op jit(solution)/shard_map/ppermute | solution.py:368
  22.5 0.0 collective-permute-done.4.refs_3_
  22.5 0.9 %collective-permute-start.9 = (bf16[8,64,256]{2,1,0:T(8,128)(2,1)S(1)}, bf16[8,64,256]{2,1,0:T(8,128)(2,1)S(1)}, u32[]{:S(2)}, u32[]{:S(2)}) collective-permute-start(bf16[8,64,256]{2,1,0:T(8,128)(2,1)S(1)} %collective-permute-done.1.refs_1_), channel_id=1, source_target_pairs={{0,16},{4,20},{8,24},{12,28},{16,0},{20,4},{24,8},{28,12},{1,17},{... | collective-permute-start | bytes 786440 | tf_op jit(solution)/shard_map/ppermute | solution.py:368
  23.4 0.7 %pad_add_fusion.ints = s32[9,272]{1,0:T(8,128)S(1)} fusion(s32[1,256]{1,0:T(1,128)} %param.9, s32[8,16]{1,0:T(8,128)} %param.6, s32[8,256]{1,0:T(8,128)} %param.8), kind=kLoop, calls=%fused_computation | loop fusion | flops 4896 | bytes 19520 | tf_op jit(solution)/shard_map/concatenate | solution.py:388
  24.1 0.0 collective-permute-done.5.refs_4_
  24.1 1.6 %collective-permute-start.7 = (s32[9,272]{1,0:T(8,128)S(1)}, s32[9,272]{1,0:T(8,128)S(1)}, u32[]{:S(2)}, u32[]{:S(2)}) collective-permute-start(s32[9,272]{1,0:T(8,128)S(1)} %pad_add_fusion.ints), channel_id=1, source_target_pairs={{1,0},{3,1},{0,2},{2,3},{5,4},{7,5},{4,6},{6,7},{9,8},{11,9},{8,10... | collective-permute-start | bytes 29384 | tf_op jit(solution)/shard_map/ppermute | solution.py:385
  25.7 0.0 copy-done
  25.7 0.0 copy-start.1
  25.7 0.9 %copy-done.1 = bf16[8,64,256]{2,1,0:T(8,128)(2,1)S(1)} copy-done((bf16[8,64,256]{2,1,0:T(8,128)(2,1)S(1)}, bf16[8,64,256]{2,1,0:T(8,128)(2,1)}, u32[]{:S(2)}) %copy-start.1) | copy-done | bytes 262168
  26.7 10.4 %partial_sums.2 = (bf16[2064,128]{1,0:T(8,128)(2,1)S(1)}, bf16[2064,128]{1,0:T(8,128)(2,1)}, bf16[2064,128]{1,0:T(8,128)(2,1)S(1)}, bf16[528,128]{1,0:T(8,128)(2,1)S(1)}) custom-call(s32[9,272]{1,0:T(8,128)S(1)} %pad_add_fusion.ints, bf16[8,64,1024]{2,1,0:T(8,128)(2,1)S(1)} %copy-done, bf16[8,64,256]{2,1,0:T(8,128)(2,1)S(1)} %copy-done.1, ...), custom_call_target="tpu_custom_call" | custom-call | flops 1 | bytes 1 | tf_op jit(solution)/shard_map/partial_sums/pallas_call | solution.py:190
  37.1 0.0 collective-permute-done.7.ints
  37.1 0.0 collective-permute-done.10.refs_4_
  37.1 0.0 collective-permute-done.8.refs_2_
  37.1 0.0 collective-permute-done.9.refs_3_
  37.1 0.0 collective-permute-done.6.refs_0_
  37.1 0.1 collective-permute-start.11
  37.2 0.5 collective-permute-start.12
  37.7 0.1 collective-permute-start.13
  37.8 0.4 collective-permute-start.14
  38.2 2.3 %collective-permute-start.15 = (bf16[528,128]{1,0:T(8,128)(2,1)S(1)}, bf16[528,128]{1,0:T(8,128)(2,1)S(1)}, u32[]{:S(2)}, u32[]{:S(2)}) collective-permute-start(bf16[528,128]{1,0:T(8,128)(2,1)S(1)} %get-tuple-element.35), channel_id=1, source_target_pairs={{0,3},{3,0},{4,7},{7,4},{8,11},{11,8},{12,15},{15,12},{16,19},{19,... | collective-permute-start | bytes 405512 | tf_op jit(solution)/shard_map/ppermute | solution.py:409
  40.5 0.0 collective-permute-done.11.refs_5_
  40.5 0.1 collective-permute-start.16
  40.6 0.0 collective-permute-done.12.refs_6_
  40.6 0.7 collective-permute-start.17
  41.3 0.0 collective-permute-done.13.refs_7_
  41.3 0.0 collective-permute-done.14.refs_8_
  41.3 10.6 %partial_sums.3 = (bf16[2064,128]{1,0:T(8,128)(2,1)S(1)}, bf16[1552,128]{1,0:T(8,128)(2,1)}) custom-call(s32[9,272]{1,0:T(8,128)S(1)} %collective-permute-done.7.ints, bf16[8,64,1024]{2,1,0:T(8,128)(2,1)S(1)} %collective-permute-done.6.refs_0_, bf16[8,64,256]{2,1,0:T(8,128)(2,1)S(1)} %collective-permute-done.1.refs_1_, ...), custom_call_target="tpu_custom_call" | custom-call | flops 1 | bytes 1 | tf_op jit(solution)/shard_map/partial_sums/pallas_call | solution.py:190
  51.9 0.0 collective-permute-done.15.refs_3_
  51.9 1.3 %collective-permute-start.18 = (bf16[1552,128]{1,0:T(8,128)(2,1)}, bf16[1552,128]{1,0:T(8,128)(2,1)S(1)}, u32[]{:S(2)}, u32[]{:S(2)}) collective-permute-start(bf16[1552,128]{1,0:T(8,128)(2,1)} %get-tuple-element.40), channel_id=1, source_target_pairs={{1,0},{2,3},{5,4},{6,7},{9,8},{10,11},{13,12},{14,15},{17,16},{18,... | collective-permute-start | bytes 1191944 | tf_op jit(solution)/shard_map/ppermute | solution.py:417
  53.2 0.1 pad_add_fusion.1.me_ref
  53.3 5.6 %collective-permute-done.16.refs_2_ = bf16[2064,128]{1,0:T(8,128)(2,1)S(1)} collective-permute-done((bf16[2064,128]{1,0:T(8,128)(2,1)}, bf16[2064,128]{1,0:T(8,128)(2,1)S(1)}, u32[]{:S(2)}, u32[]{:S(2)}) %collective-permute-start.16) | collective-permute-done | bytes 528416 | tf_op jit(solution)/shard_map/ppermute | solution.py:410
  58.9 2.6 %early_sums.1.table = f32[128,32,128]{2,1,0:T(8,128)S(1)} custom-call(s32[2]{0:T(128)S(1)} %pad_add_fusion.1.me_ref, bf16[2064,128]{1,0:T(8,128)(2,1)S(1)} %get-tuple-element.26.refs_0_, bf16[2064,128]{1,0:T(8,128)(2,1)S(1)} %get-tuple-element.36.refs_1_, bf16[2064,128]{1,0:T(8,128)(2,1)S(1)} %collective-permute-done.16.refs_2_, ...), custom_call_target="tpu_custom_call" | custom-call | tf_op jit(solution)/shard_map/early_sums/pallas_call | solution.py:324
  61.5 0.0 collective-permute-done.17.from_b
  61.5 5.7 %collective-permute-done.18.from_c = bf16[1552,128]{1,0:T(8,128)(2,1)S(1)} collective-permute-done((bf16[1552,128]{1,0:T(8,128)(2,1)}, bf16[1552,128]{1,0:T(8,128)(2,1)S(1)}, u32[]{:S(2)}, u32[]{:S(2)}) %collective-permute-start.18) | collective-permute-done | bytes 397344 | tf_op jit(solution)/shard_map/ppermute | solution.py:417
  67.3 3.8 %owner_sums.1 = f32[128,4096]{1,0:T(8,128)} custom-call(s32[2]{0:T(128)S(1)} %pad_add_fusion.1.me_ref, f32[128,32,128]{2,1,0:T(8,128)S(1)} %early_sums.1.table, bf16[2064,128]{1,0:T(8,128)(2,1)S(1)} %collective-permute-done.17.from_b, bf16[1552,128]{1,0:T(8,128)(2,1)S(1)} %collective-permute-done.18.from_c), custom_call_target="tpu_custom_call" | custom-call | tf_op jit(solution)/shard_map/owner_sums/pallas_call | solution.py:344
  (3 shorter events, 0.1 us)
Async XLA Ops:
  0.0 25.7 %copy-start = (bf16[8,64,1024]{2,1,0:T(8,128)(2,1)S(1)}, bf16[8,64,1024]{2,1,0:T(8,128)(2,1)}, u32[]{:S(2)}) copy-start(bf16[8,64,1024]{2,1,0:T(8,128)(2,1)} %refs_0_.1) | copy-start | bytes 3145732
  0.0 10.0 %collective-permute-start = (bf16[8,64,256]{2,1,0:T(8,128)(2,1)}, bf16[8,64,256]{2,1,0:T(8,128)(2,1)S(1)}, u32[]{:S(2)}, u32[]{:S(2)}) collective-permute-start(bf16[8,64,256]{2,1,0:T(8,128)(2,1)} %refs_1_.1), channel_id=1, source_target_pairs={{0,8},{4,12},{8,0},{12,4},{16,24},{20,28},{24,16},{28,20},{1,9},{5... | collective-permute-start | bytes 786440 | tf_op jit(solution)/shard_map/ppermute | solution.py:368
  2.9 9.7 %collective-permute-start.1 = (bf16[8,64,256]{2,1,0:T(8,128)(2,1)}, bf16[8,64,256]{2,1,0:T(8,128)(2,1)S(1)}, u32[]{:S(2)}, u32[]{:S(2)}) collective-permute-start(bf16[8,64,256]{2,1,0:T(8,128)(2,1)} %refs_1_.1), channel_id=1, source_target_pairs={{1,0},{3,1},{0,2},{2,3},{5,4},{7,5},{4,6},{6,7},{9,8},{11,9},{8,10... | collective-permute-start | bytes 786440 | tf_op jit(solution)/shard_map/ppermute | solution.py:385
  5.5 13.3 %collective-permute-start.2 = (bf16[8,64,256]{2,1,0:T(8,128)(2,1)}, bf16[8,64,256]{2,1,0:T(8,128)(2,1)S(1)}, u32[]{:S(2)}, u32[]{:S(2)}) collective-permute-start(bf16[8,64,256]{2,1,0:T(8,128)(2,1)} %refs_1_.1), channel_id=1, source_target_pairs={{0,16},{4,20},{8,24},{12,28},{16,0},{20,4},{24,8},{28,12},{1,17},{... | collective-permute-start | bytes 786440 | tf_op jit(solution)/shard_map/ppermute | solution.py:368
  7.1 11.8 %collective-permute-start.3 = (bf16[8,64,256]{2,1,0:T(8,128)(2,1)}, bf16[8,64,256]{2,1,0:T(8,128)(2,1)S(1)}, u32[]{:S(2)}, u32[]{:S(2)}) collective-permute-start(bf16[8,64,256]{2,1,0:T(8,128)(2,1)} %refs_1_.1), channel_id=1, source_target_pairs={{0,24},{4,28},{8,16},{12,20},{16,8},{20,12},{24,0},{28,4},{1,25},{... | collective-permute-start | bytes 786440 | tf_op jit(solution)/shard_map/ppermute | solution.py:368
  7.5 29.6 %collective-permute-start.6 = (bf16[8,64,1024]{2,1,0:T(8,128)(2,1)}, bf16[8,64,1024]{2,1,0:T(8,128)(2,1)S(1)}, u32[]{:S(2)}, u32[]{:S(2)}) collective-permute-start(bf16[8,64,1024]{2,1,0:T(8,128)(2,1)} %refs_0_.1), channel_id=1, source_target_pairs={{1,0},{3,1},{0,2},{2,3},{5,4},{7,5},{4,6},{6,7},{9,8},{11,9},{8,10... | collective-permute-start | bytes 3145736 | tf_op jit(solution)/shard_map/ppermute | solution.py:385
  18.9 5.2 %collective-permute-start.5 = (bf16[24,64,256]{2,1,0:T(8,128)(2,1)S(1)}, bf16[24,64,256]{2,1,0:T(8,128)(2,1)S(1)}, u32[]{:S(2)}, u32[]{:S(2)}) collective-permute-start(bf16[24,64,256]{2,1,0:T(8,128)(2,1)S(1)} %constant_dynamic-update-slice_fusion.refs_2_), channel_id=1, source_target_pairs={{0,4},{4,0},{8,12},{12,8},{16,20},{20,16},{24,28},{28,24},{1,5},{5... | collective-permute-start | bytes 2359304 | tf_op jit(solution)/shard_map/ppermute | solution.py:368
  19.0 3.5 %collective-permute-start.4 = (bf16[8,64,256]{2,1,0:T(8,128)(2,1)}, bf16[8,64,256]{2,1,0:T(8,128)(2,1)S(1)}, u32[]{:S(2)}, u32[]{:S(2)}) collective-permute-start(bf16[8,64,256]{2,1,0:T(8,128)(2,1)} %refs_1_.1), channel_id=1, source_target_pairs={{0,4},{4,0},{8,12},{12,8},{16,20},{20,16},{24,28},{28,24},{1,5},{5... | collective-permute-start | bytes 786440 | tf_op jit(solution)/shard_map/ppermute | solution.py:368
  19.5 17.6 %collective-permute-start.10 = (bf16[8,64,256]{2,1,0:T(8,128)(2,1)S(1)}, bf16[8,64,256]{2,1,0:T(8,128)(2,1)S(1)}, u32[]{:S(2)}, u32[]{:S(2)}) collective-permute-start(bf16[8,64,256]{2,1,0:T(8,128)(2,1)S(1)} %collective-permute-done.1.refs_1_), channel_id=1, source_target_pairs={{0,24},{4,28},{8,16},{12,20},{16,8},{20,12},{24,0},{28,4},{1,25},{... | collective-permute-start | bytes 786440 | tf_op jit(solution)/shard_map/ppermute | solution.py:368
  21.0 16.1 %collective-permute-start.8 = (bf16[8,64,256]{2,1,0:T(8,128)(2,1)S(1)}, bf16[8,64,256]{2,1,0:T(8,128)(2,1)S(1)}, u32[]{:S(2)}, u32[]{:S(2)}) collective-permute-start(bf16[8,64,256]{2,1,0:T(8,128)(2,1)S(1)} %collective-permute-done.1.refs_1_), channel_id=1, source_target_pairs={{0,8},{4,12},{8,0},{12,4},{16,24},{20,28},{24,16},{28,20},{1,9},{5... | collective-permute-start | bytes 786440 | tf_op jit(solution)/shard_map/ppermute | solution.py:368
  22.5 14.7 %collective-permute-start.9 = (bf16[8,64,256]{2,1,0:T(8,128)(2,1)S(1)}, bf16[8,64,256]{2,1,0:T(8,128)(2,1)S(1)}, u32[]{:S(2)}, u32[]{:S(2)}) collective-permute-start(bf16[8,64,256]{2,1,0:T(8,128)(2,1)S(1)} %collective-permute-done.1.refs_1_), channel_id=1, source_target_pairs={{0,16},{4,20},{8,24},{12,28},{16,0},{20,4},{24,8},{28,12},{1,17},{... | collective-permute-start | bytes 786440 | tf_op jit(solution)/shard_map/ppermute | solution.py:368
  24.1 13.0 %collective-permute-start.7 = (s32[9,272]{1,0:T(8,128)S(1)}, s32[9,272]{1,0:T(8,128)S(1)}, u32[]{:S(2)}, u32[]{:S(2)}) collective-permute-start(s32[9,272]{1,0:T(8,128)S(1)} %pad_add_fusion.ints), channel_id=1, source_target_pairs={{1,0},{3,1},{0,2},{2,3},{5,4},{7,5},{4,6},{6,7},{9,8},{11,9},{8,10... | collective-permute-start | bytes 29384 | tf_op jit(solution)/shard_map/ppermute | solution.py:385
  25.7 1.0 %copy-start.1 = (bf16[8,64,256]{2,1,0:T(8,128)(2,1)S(1)}, bf16[8,64,256]{2,1,0:T(8,128)(2,1)}, u32[]{:S(2)}) copy-start(bf16[8,64,256]{2,1,0:T(8,128)(2,1)} %refs_1_.1) | copy-start | bytes 786436
  37.1 3.4 %collective-permute-start.11 = (bf16[8,64,256]{2,1,0:T(8,128)(2,1)S(1)}, bf16[8,64,256]{2,1,0:T(8,128)(2,1)S(1)}, u32[]{:S(2)}, u32[]{:S(2)}) collective-permute-start(bf16[8,64,256]{2,1,0:T(8,128)(2,1)S(1)} %collective-permute-done.1.refs_1_), channel_id=1, source_target_pairs={{0,4},{4,0},{8,12},{12,8},{16,20},{20,16},{24,28},{28,24},{1,5},{5... | collective-permute-start | bytes 786440 | tf_op jit(solution)/shard_map/ppermute | solution.py:368
  37.2 3.4 %collective-permute-start.12 = (bf16[8,64,256]{2,1,0:T(8,128)(2,1)S(1)}, bf16[8,64,256]{2,1,0:T(8,128)(2,1)S(1)}, u32[]{:S(2)}, u32[]{:S(2)}) collective-permute-start(bf16[8,64,256]{2,1,0:T(8,128)(2,1)S(1)} %collective-permute-done.8.refs_2_), channel_id=1, source_target_pairs={{0,4},{4,0},{8,12},{12,8},{16,20},{20,16},{24,28},{28,24},{1,5},{5... | collective-permute-start | bytes 786440 | tf_op jit(solution)/shard_map/ppermute | solution.py:368
  37.7 3.6 %collective-permute-start.13 = (bf16[8,64,256]{2,1,0:T(8,128)(2,1)S(1)}, bf16[8,64,256]{2,1,0:T(8,128)(2,1)S(1)}, u32[]{:S(2)}, u32[]{:S(2)}) collective-permute-start(bf16[8,64,256]{2,1,0:T(8,128)(2,1)S(1)} %collective-permute-done.9.refs_3_), channel_id=1, source_target_pairs={{0,4},{4,0},{8,12},{12,8},{16,20},{20,16},{24,28},{28,24},{1,5},{5... | collective-permute-start | bytes 786440 | tf_op jit(solution)/shard_map/ppermute | solution.py:368
  37.8 3.5 %collective-permute-start.14 = (bf16[8,64,256]{2,1,0:T(8,128)(2,1)S(1)}, bf16[8,64,256]{2,1,0:T(8,128)(2,1)S(1)}, u32[]{:S(2)}, u32[]{:S(2)}) collective-permute-start(bf16[8,64,256]{2,1,0:T(8,128)(2,1)S(1)} %collective-permute-done.10.refs_4_), channel_id=1, source_target_pairs={{0,4},{4,0},{8,12},{12,8},{16,20},{20,16},{24,28},{28,24},{1,5},{5... | collective-permute-start | bytes 786440 | tf_op jit(solution)/shard_map/ppermute | solution.py:368
  38.2 13.7 %collective-permute-start.15 = (bf16[528,128]{1,0:T(8,128)(2,1)S(1)}, bf16[528,128]{1,0:T(8,128)(2,1)S(1)}, u32[]{:S(2)}, u32[]{:S(2)}) collective-permute-start(bf16[528,128]{1,0:T(8,128)(2,1)S(1)} %get-tuple-element.35), channel_id=1, source_target_pairs={{0,3},{3,0},{4,7},{7,4},{8,11},{11,8},{12,15},{15,12},{16,19},{19,... | collective-permute-start | bytes 405512 | tf_op jit(solution)/shard_map/ppermute | solution.py:409
  40.5 18.4 %collective-permute-start.16 = (bf16[2064,128]{1,0:T(8,128)(2,1)}, bf16[2064,128]{1,0:T(8,128)(2,1)S(1)}, u32[]{:S(2)}, u32[]{:S(2)}) collective-permute-start(bf16[2064,128]{1,0:T(8,128)(2,1)} %get-tuple-element.37), channel_id=1, source_target_pairs={{0,1},{3,2},{1,3},{2,0},{4,5},{7,6},{5,7},{6,4},{8,9},{11,10},{9,1... | collective-permute-start | bytes 1585160 | tf_op jit(solution)/shard_map/ppermute | solution.py:410
  40.6 20.9 %collective-permute-start.17 = (bf16[2064,128]{1,0:T(8,128)(2,1)S(1)}, bf16[2064,128]{1,0:T(8,128)(2,1)S(1)}, u32[]{:S(2)}, u32[]{:S(2)}) collective-permute-start(bf16[2064,128]{1,0:T(8,128)(2,1)S(1)} %get-tuple-element.39), channel_id=1, source_target_pairs={{1,2},{2,1},{5,6},{6,5},{9,10},{10,9},{13,14},{14,13},{17,18},{18,... | collective-permute-start | bytes 1585160 | tf_op jit(solution)/shard_map/ppermute | solution.py:411
  51.9 15.3 %collective-permute-start.18 = (bf16[1552,128]{1,0:T(8,128)(2,1)}, bf16[1552,128]{1,0:T(8,128)(2,1)S(1)}, u32[]{:S(2)}, u32[]{:S(2)}) collective-permute-start(bf16[1552,128]{1,0:T(8,128)(2,1)} %get-tuple-element.40), channel_id=1, source_target_pairs={{1,0},{2,3},{5,4},{6,7},{9,8},{10,11},{13,12},{14,15},{17,16},{18,... | collective-permute-start | bytes 1191944 | tf_op jit(solution)/shard_map/ppermute | solution.py:417
